TPU v7x, 128 devices: a whole 4x4x4 slice. The times are simulated.
128 devices in a mesh: tm: 4 (over x), rows: 32 (over y, z, core).
Axes of the slice: x: 4, y: 4, z: 4, core: 2. Of those that a mesh axis runs over, the one named last changes fastest.
Arguments:
- frames: bfloat16 [16, 256, 1280, 128], P('tm', 'rows'), may hold values from -30 to 30
- clip_ids: int32 [16], replicated, may hold values from 0 to 3, never falling along the last dimension, each value on 1 to 6 neighbouring positions
- conv_weight: bfloat16 [3, 3, 3, 128, 256], replicated, may hold values from -0.109375 to 0.109375
- norm_gain: float32 [256], replicated, may hold values from 0.1 to 1.9
- norm_bias: float32 [256], replicated, may hold values from -3 to 3
Outputs:
- latent: bfloat16 [16, 128, 640, 256], P('tm', None, 'rows')
Inputs may be any that keep to these rules, and one draw needn't show every extreme that they name: `clip_ids`: clip numbers never fall along the frames; each clip spans 1 to 6 frames, one exactly 6.
All inputs are finite; a program needn't handle non-finite values.
Results may differ from a plain program's by a relative error of at most 0.012.
Values may be sent and summed in bfloat16 or wider, within the bound.
A program may use at most 192 MiB of HBM per device.

v0:
```python
import jax
import jax.numpy as jnp
from jax import lax
from jax.sharding import PartitionSpec as P

GROUPS = 32


def passed_along(array, axis, by):
    length = lax.axis_size(axis)
    pairs = [(i, i + by) for i in range(length) if 0 <= i + by < length]
    return lax.ppermute(array, axis, pairs)


def conv_tap(source, kernel):
    return lax.conv_general_dilated(
        source,
        kernel,
        (2, 2),
        ((0, 0), (1, 1)),
        dimension_numbers=("NHWC", "HWIO", "NHWC"),
        preferred_element_type=jnp.float32,
    )


def group_sums(block):
    values = block.astype(jnp.float32).reshape(
        block.shape[0], block.shape[1], block.shape[2], GROUPS, -1
    )
    return (jnp.sum(values, axis=(1, 2, 4)), jnp.sum(values * values, axis=(1, 2, 4)))


def finish(block, sum_first, sum_second, norm_gain, norm_bias):
    values = block.astype(jnp.float32).reshape(
        block.shape[0], block.shape[1], block.shape[2], GROUPS, -1
    )
    entries = block.shape[1] * block.shape[2] * values.shape[4] * lax.axis_size("rows")
    mean = sum_first / entries
    variance = sum_second / entries - mean * mean
    scaled = (values - mean[:, None, None, :, None]) * lax.rsqrt(variance + 1e-05)[
        :, None, None, :, None
    ]
    scaled = scaled.reshape(block.shape) * norm_gain + norm_bias
    return jax.nn.silu(scaled).astype(jnp.bfloat16)


def on_device(frames, clip_ids, conv_weight, norm_gain, norm_bias):
    frame_count = frames.shape[0]
    row_above = passed_along(frames[:, -1:], "rows", 1)
    extended = jnp.concatenate([row_above, frames], axis=1)
    stretch_start = lax.axis_index("tm") * frame_count
    sentinel = jnp.full((2,), -1, jnp.int32)
    padded = jnp.concatenate([sentinel, clip_ids, sentinel])
    window = lax.dynamic_slice_in_dim(padded, stretch_start, frame_count + 4)
    target = window[2 : frame_count + 2]
    running = jnp.zeros(
        (frame_count, frames.shape[1] // 2, frames.shape[2] // 2, conv_weight.shape[4]), jnp.float32
    )
    history_head = passed_along(extended[-2:], "tm", 1)
    history = jnp.concatenate([history_head, extended], axis=0)
    for tap_index in range(3):
        keep_mask = (window[tap_index : tap_index + frame_count] == target).astype(frames.dtype)
        running = running + conv_tap(
            history[tap_index : tap_index + frame_count] * keep_mask[:, None, None, None],
            conv_weight[tap_index],
        )
    conv = running.astype(jnp.bfloat16)
    sum_first, sum_second = lax.psum(group_sums(conv), "rows")
    banded = finish(conv, sum_first, sum_second, norm_gain, norm_bias)
    return lax.all_to_all(banded, "rows", split_axis=2, concat_axis=1, tiled=True)


def solution(mesh):
    in_specs = (P("tm", "rows", None, None), P(), P(), P(), P())
    out_specs = P("tm", None, "rows", None)
    return jax.shard_map(
        on_device, mesh=mesh, in_specs=in_specs, out_specs=out_specs, check_vma=False
    )
```

profile of v0, /device:TPU:1, one launch (start us, length us, event | category | flops | bytes accessed | tf_op | source)
XLA Modules:
  0.0 470.1 jit_solution(5616610376107157981)
XLA Ops:
  0.0 1.4 slice.31
  1.4 4.9 %collective-permute-start = (bf16[4,1,1280,128]{3,2,1,0:T(8,128)(2,1)S(1)}, bf16[4,1,1280,128]{3,2,1,0:T(8,128)(2,1)S(1)}, u32[]{:S(2)}, u32[]{:S(2)}) collective-permute-start(bf16[4,1,1280,128]{3,2,1,0:T(8,128)(2,1)S(1)} %slice.31), channel_id=1, source_target_pairs={{0,1},{1,2},{2,3},{3,4},{4,5},{5,6},{6,7},{7,8},{8,9},{9,10},{10,1... | collective-permute-start | bytes 3932168 | tf_op jit(solution)/shard_map/ppermute | solution.py:12
  6.3 14.5 %collective-permute-done = bf16[4,1,1280,128]{3,2,1,0:T(8,128)(2,1)S(1)} collective-permute-done((bf16[4,1,1280,128]{3,2,1,0:T(8,128)(2,1)S(1)}, bf16[4,1,1280,128]{3,2,1,0:T(8,128)(2,1)S(1)}, u32[]{:S(2)}, u32[]{:S(2)}) %collective-permute-start) | collective-permute-done | bytes 1310752 | tf_op jit(solution)/shard_map/ppermute | solution.py:12
  20.9 1.3 constant_dynamic-update-slice_fusion.1
  22.2 10.8 %constant_dynamic-update-slice_fusion = bf16[4,9,1280,128]{3,2,1,0:T(8,128)(2,1)} fusion(bf16[4,9,1280,128]{3,2,1,0:T(8,128)(2,1)} %constant_dynamic-update-slice_fusion.1, bf16[4,8,1280,128]{3,2,1,0:T(8,128)(2,1)} %param.5), kind=kLoop, calls=%fused_computation.40 | loop fusion | bytes 20971520 | tf_op jit(solution)/shard_map/concatenate | solution.py:50
  33.0 5.7 %slice.47 = bf16[2,9,1280,128]{3,2,1,0:T(8,128)(2,1)} slice(bf16[4,9,1280,128]{3,2,1,0:T(8,128)(2,1)} %constant_dynamic-update-slice_fusion), slice={[2:4], [0:9], [0:1280], [0:128]} | slice | bytes 11796480 | tf_op jit(solution)/shard_map/slice | solution.py:59
  38.7 5.9 %collective-permute-start.1 = (bf16[2,9,1280,128]{3,2,1,0:T(8,128)(2,1)}, bf16[2,9,1280,128]{3,2,1,0:T(8,128)(2,1)}, u32[]{:S(2)}, u32[]{:S(2)}) collective-permute-start(bf16[2,9,1280,128]{3,2,1,0:T(8,128)(2,1)} %slice.47), channel_id=1, source_target_pairs={{0,32},{32,64},{64,96},{1,33},{33,65},{65,97},{2,34},{34,66},{66,9... | collective-permute-start | bytes 17694728 | tf_op jit(solution)/shard_map/ppermute | solution.py:12
  44.6 0.0 copy-done.3
  44.6 0.1 pad_add_fusion
  44.7 0.1 dynamic_slice.3
  44.7 0.1 compare_convert_fusion.1
  44.8 11.0 %pad.4 = bf16[9,4,1296,128]{3,2,0,1:T(8,128)(2,1)} pad(bf16[9,4,1280,128]{3,2,0,1:T(8,128)(2,1)} %bitcast.52, bf16[]{:T(256)} %constant.28), padding=0_0x0_0x1_15x0_0 | pad | bytes 23740418 | tf_op jit(solution)/shard_map/concatenate | solution.py:50
  55.8 15.4 %reshape.47 = bf16[9,4,8,162,128]{4,3,2,0,1:T(8,128)(2,1)} reshape(bf16[9,4,1296,128]{3,2,0,1:T(8,128)(2,1)} %pad.4) | data formatting | bytes 23887872 | tf_op jit(solution)/shard_map/conv_general_dilated | solution.py:16
  71.2 1.1 slice.52
  72.4 0.1 copy.89
  72.5 0.0 copy-start.2
  72.5 0.0 slice-start
  72.5 0.0 slice-start.1
  72.5 7.7 %fusion.5 = bf16[9,4,8,164,128]{4,3,2,1,0:T(8,128)(2,1)S(1)} fusion(bf16[9,4,7,2,128]{4,3,2,1,0:T(2,128)(2,1)S(1)} %copy.89, bf16[9,4,8,162,128]{4,3,2,0,1:T(8,128)(2,1)} %reshape.47), kind=kLoop, calls=%fused_computation.8 | loop fusion | flops 36274176 | bytes 24164352 | tf_op jit(solution)/shard_map/conv_general_dilated | solution.py:16
  80.3 0.0 copy-done.2
  80.3 0.0 slice-start.2
  80.3 12.1 %fusion.6 = f32[4,32,81,256]{3,1,2,0:T(8,128)} fusion(bf16[9,4,8,164,128]{4,3,2,1,0:T(8,128)(2,1)S(1)} %fusion.5, bf16[3,3,3,128,256]{4,3,2,1,0:T(8,128)(2,1)S(1)} %copy-done.2), kind=kOutput, calls=%fused_computation.9 | convolution fusion | flops 6115295232 | bytes 23592960 | tf_op jit(solution)/shard_map/conv_general_dilated | solution.py:16
  92.4 63.5 %collective-permute-done.1 = bf16[2,9,1280,128]{3,2,1,0:T(8,128)(2,1)} collective-permute-done((bf16[2,9,1280,128]{3,2,1,0:T(8,128)(2,1)}, bf16[2,9,1280,128]{3,2,1,0:T(8,128)(2,1)}, u32[]{:S(2)}, u32[]{:S(2)}) %collective-permute-start.1) | collective-permute-done | bytes 5898272 | tf_op jit(solution)/shard_map/ppermute | solution.py:12
  155.9 0.0 slice-done
  155.9 0.0 slice-done.1
  155.9 9.6 %fusion.17 = (bf16[9,4,1280,128]{3,2,0,1:T(8,128)(2,1)S(1)}, bf16[9,4,1280,128]{3,2,0,1:T(8,128)(2,1)}) fusion(bf16[2,9,1280,128]{3,2,1,0:T(8,128)(2,1)} %collective-permute-done.1, bf16[4,9,1280,128]{3,2,1,0:T(8,128)(2,1)S(1)} %bitcast.54, bf16[4]{0:T(256)(128)(2,1)S(1)} %get-tuple-element.11, bf16[4]{0:T(256)(128)(2,1)S(1)} %get-tuple-element.12), kind=kLoop, calls=%fused_computation.20 | loop fusion | flops 23592960 | bytes 41287696 | tf_op jit(solution)/shard_map/mul | solution.py:64
  165.5 6.1 %pad = bf16[9,4,1296,128]{3,2,0,1:T(8,128)(2,1)} pad(bf16[9,4,1280,128]{3,2,0,1:T(8,128)(2,1)S(1)} %get-tuple-element.7, bf16[]{:T(256)} %constant.28), padding=0_0x0_0x1_15x0_0 | pad | bytes 23740418 | tf_op jit(solution)/shard_map/mul | solution.py:64
  171.6 15.4 %reshape.45 = bf16[9,4,8,162,128]{4,3,2,0,1:T(8,128)(2,1)} reshape(bf16[9,4,1296,128]{3,2,0,1:T(8,128)(2,1)} %pad) | data formatting | bytes 23887872 | tf_op jit(solution)/shard_map/conv_general_dilated | solution.py:16
  187.0 1.1 slice.50
  188.2 0.1 copy.91
  188.3 11.1 %fusion.3 = bf16[9,4,8,164,128]{4,3,2,1,0:T(8,128)(2,1)} fusion(bf16[9,4,7,2,128]{4,3,2,1,0:T(2,128)(2,1)S(1)} %copy.91, bf16[9,4,8,162,128]{4,3,2,0,1:T(8,128)(2,1)} %reshape.45), kind=kLoop, calls=%fused_computation.6 | loop fusion | flops 36274176 | bytes 24164352 | tf_op jit(solution)/shard_map/conv_general_dilated | solution.py:16
  199.3 11.0 %pad.2 = bf16[9,4,1296,128]{3,2,0,1:T(8,128)(2,1)} pad(bf16[9,4,1280,128]{3,2,0,1:T(8,128)(2,1)} %get-tuple-element.8, bf16[]{:T(256)} %constant.28), padding=0_0x0_0x1_15x0_0 | pad | bytes 23740418 | tf_op jit(solution)/shard_map/mul | solution.py:64
  210.3 15.5 %reshape.46 = bf16[9,4,8,162,128]{4,3,2,0,1:T(8,128)(2,1)} reshape(bf16[9,4,1296,128]{3,2,0,1:T(8,128)(2,1)} %pad.2) | data formatting | bytes 23887872 | tf_op jit(solution)/shard_map/conv_general_dilated | solution.py:16
  225.7 1.1 slice.51
  226.9 0.1 copy.90
  227.0 6.2 %fusion.4 = bf16[9,4,8,164,128]{4,3,2,1,0:T(8,128)(2,1)S(1)} fusion(bf16[9,4,7,2,128]{4,3,2,1,0:T(2,128)(2,1)S(1)} %copy.90, bf16[9,4,8,162,128]{4,3,2,0,1:T(8,128)(2,1)} %reshape.46), kind=kLoop, calls=%fused_computation.7 | loop fusion | flops 36274176 | bytes 24164352 | tf_op jit(solution)/shard_map/conv_general_dilated | solution.py:16
  233.2 0.0 copy-start.4
  233.2 12.0 %fusion.8 = f32[4,32,81,256]{3,1,2,0:T(8,128)} fusion(bf16[9,4,8,164,128]{4,3,2,1,0:T(8,128)(2,1)S(1)} %fusion.4, bf16[3,3,3,128,256]{4,3,2,1,0:T(8,128)(2,1)S(1)} %copy-done.2), kind=kOutput, calls=%fused_computation.11 | convolution fusion | flops 6115295232 | bytes 23592960 | tf_op jit(solution)/shard_map/conv_general_dilated | solution.py:16
  245.3 19.6 %fusion.31 = (f32[4,32,81,256]{3,1,2,0:T(8,128)}, f32[4,32,81,256]{3,1,2,0:T(8,128)}) fusion(f32[4,32,81,256]{3,1,2,0:T(8,128)} %fusion.6, f32[4,32,81,256]{3,1,2,0:T(8,128)} %fusion.8, bf16[3,3,3,128,256]{4,3,2,1,0:T(8,128)(2,1)S(1)} %copy-done.2, bf16[9,4,8,164,128]{4,3,2,1,0:T(8,128)(2,1)} %fusion.3, pred[32,81]{0,1:T(8,128)(4,1)S(1)} %copy-done.4), kind=kOutput, calls=%fused_computation.47 | convolution fusion | flops 6136528896 | bytes 55159808 | tf_op jit(solution)/shard_map/conv_general_dilated | solution.py:16
  264.9 12.6 %copy.42 = f32[4,32,81,256]{3,0,2,1:T(4,128)S(1)} copy(f32[4,32,81,256]{3,1,2,0:T(8,128)} %get-tuple-element.14) | data formatting | bytes 21233664 | tf_op jit(solution)/shard_map/convert_element_type | solution.py:34
  277.5 1.0 slice_reduce_fusion.1
  278.4 0.1 reduce_sum.24
  278.5 12.6 %copy.44 = f32[4,32,81,256]{3,0,2,1:T(4,128)S(1)} copy(f32[4,32,81,256]{3,1,2,0:T(8,128)} %get-tuple-element.13) | data formatting | bytes 21233664 | tf_op jit(solution)/shard_map/mul | solution.py:30
  291.1 1.0 slice_reduce_fusion
  292.1 0.0 copy-start
  292.1 0.0 copy-start.1
  292.2 0.1 reduce_sum.36
  292.2 0.1 reduce_sum.25
  292.3 0.1 reduce_sum.37
  292.4 72.0 %all-reduce = (f32[4,32]{1,0:T(4,128)S(1)}, f32[4,32]{1,0:T(4,128)S(1)}) all-reduce(f32[4,32]{1,0:T(4,128)S(1)} %reduce_sum.37, f32[4,32]{1,0:T(4,128)S(1)} %reduce_sum.25), channel_id=1, replica_groups=mesh['tm'=4,'rows'=32] {'rows'}, use_global_device_ids=true, to_apply=%region_5.6 | all-reduce | flops 256 | bytes 2048 | tf_op jit(solution)/shard_map/psum | solution.py:68
  364.5 0.1 sub.16
  364.6 0.1 sub.17
  364.7 0.1 mul.62
  364.8 0.1 mul.63
  364.9 1.4 broadcast.34
  366.2 5.4 %broadcast.35 = f32[4,4,648,256]{3,0,2,1:T(4,128)} broadcast(f32[4,256]{1,0:T(4,128)S(1)} %mul.63), dimensions={1,3} | broadcast | bytes 10620928 | tf_op jit(solution)/shard_map/mul | solution.py:40
  371.6 0.0 copy-done.1
  371.6 12.8 %multiply_convert_fusion = bf16[4,32,81,256]{3,1,2,0:T(8,128)(2,1)} fusion(f32[4,32,81,256]{3,0,2,1:T(4,128)} %bitcast.56, f32[4,32,81,256]{3,1,2,0:T(8,128)} %get-tuple-element.14, f32[4,32,81,256]{3,0,2,1:T(4,128)S(1)} %bitcast.55, f32[256]{0:T(256)S(1)} %copy-done, f32[256]{0:T(256)S(1)} %copy-done.1), kind=kLoop, calls=%fused_computation.28 | loop fusion | flops 23887872 | bytes 37160960 | tf_op jit(solution)/shard_map/convert_element_type | solution.py:44
  384.4 6.6 %copy.46 = bf16[4,32,81,256]{3,0,2,1:T(4,128)(2,1)S(1)} copy(bf16[4,32,81,256]{3,1,2,0:T(8,128)(2,1)} %multiply_convert_fusion) | data formatting | bytes 10616832 | tf_op jit(solution)/shard_map/convert_element_type | solution.py:44
  391.0 1.8 slice_bitcast_fusion
  392.8 1.8 copy.47
  394.6 68.1 %all_to_all.18 = bf16[4,4,640,256]{3,1,0,2:T(4,128)(2,1)S(1)} all-to-all(bf16[4,4,640,256]{3,1,0,2:T(4,128)(2,1)S(1)} %copy.47), channel_id=1, replica_groups=mesh['tm'=4,'rows'=32] {'rows'}, dimensions={2} | all-to-all | bytes 10485760 | tf_op jit(solution)/shard_map/all_to_all | solution.py:70
  462.8 2.8 copy.49
  465.6 4.2 copy.50
  (7 shorter events, 0.0 us)
Async XLA Ops:
  1.4 19.5 %collective-permute-start = (bf16[4,1,1280,128]{3,2,1,0:T(8,128)(2,1)S(1)}, bf16[4,1,1280,128]{3,2,1,0:T(8,128)(2,1)S(1)}, u32[]{:S(2)}, u32[]{:S(2)}) collective-permute-start(bf16[4,1,1280,128]{3,2,1,0:T(8,128)(2,1)S(1)} %slice.31), channel_id=1, source_target_pairs={{0,1},{1,2},{2,3},{3,4},{4,5},{5,6},{6,7},{7,8},{8,9},{9,10},{10,1... | collective-permute-start | bytes 3932168 | tf_op jit(solution)/shard_map/ppermute | solution.py:12
  22.2 22.4 %copy-start.3 = (s32[16]{0:T(128)S(1)}, s32[16]{0:T(128)}, u32[]{:S(2)}) copy-start(s32[16]{0:T(128)} %param.6) | copy-start | bytes 196
  38.7 117.2 %collective-permute-start.1 = (bf16[2,9,1280,128]{3,2,1,0:T(8,128)(2,1)}, bf16[2,9,1280,128]{3,2,1,0:T(8,128)(2,1)}, u32[]{:S(2)}, u32[]{:S(2)}) collective-permute-start(bf16[2,9,1280,128]{3,2,1,0:T(8,128)(2,1)} %slice.47), channel_id=1, source_target_pairs={{0,32},{32,64},{64,96},{1,33},{33,65},{65,97},{2,34},{34,66},{66,9... | collective-permute-start | bytes 17694728 | tf_op jit(solution)/shard_map/ppermute | solution.py:12
  72.5 7.8 %copy-start.2 = (bf16[3,3,3,128,256]{4,3,2,1,0:T(8,128)(2,1)S(1)}, bf16[3,3,3,128,256]{4,3,2,1,0:T(8,128)(2,1)}, u32[]{:S(2)}) copy-start(bf16[3,3,3,128,256]{4,3,2,1,0:T(8,128)(2,1)} %param.7) | copy-start | bytes 5308420
  72.5 83.4 %slice-start = ((s8[11796480]{0:T(1024)(128)(4,1)}), s8[4194304]{0:T(1024)(128)(4,1)S(1)}, s32[]{:S(2)}) async-start(s8[11796480]{0:T(1024)(128)(4,1)} %bitcast.53), calls=%async_computation.1 | async-start | bytes 8388608
  72.5 83.4 %slice-start.1 = ((s8[11796480]{0:T(1024)(128)(4,1)}), s8[4194304]{0:T(1024)(128)(4,1)S(1)}, s32[]{:S(2)}) async-start(s8[11796480]{0:T(1024)(128)(4,1)} %bitcast.53), calls=%async_computation.2 | async-start | bytes 8388608
  80.3 75.6 %slice-start.2 = ((s8[11796480]{0:T(1024)(128)(4,1)}), s8[3407872]{0:T(1024)(128)(4,1)S(1)}, s32[]{:S(2)}) async-start(s8[11796480]{0:T(1024)(128)(4,1)} %bitcast.53), calls=%async_computation.3 | async-start | bytes 6815744
  233.2 12.1 %copy-start.4 = (pred[32,81]{0,1:T(8,128)(4,1)S(1)}, pred[32,81]{0,1:T(8,128)(4,1)}, u32[]{:S(2)}) copy-start(pred[32,81]{0,1:T(8,128)(4,1)} %constant.40) | copy-start | bytes 7780
  292.1 79.5 %copy-start = (f32[256]{0:T(256)S(1)}, f32[256]{0:T(256)}, u32[]{:S(2)}) copy-start(f32[256]{0:T(256)} %param.9) | copy-start | bytes 3076
  292.1 79.5 %copy-start.1 = (f32[256]{0:T(256)S(1)}, f32[256]{0:T(256)}, u32[]{:S(2)}) copy-start(f32[256]{0:T(256)} %param.8) | copy-start | bytes 3076
where the time goes:
time: 475 us; the launch traced here: 470 us
  local copies, waits for them, and re-layouts  147 us (31%)
  blocking collectives  140 us (29%)
  waiting for transfers between devices  78 us (16%)
  other arithmetic  49.7 us (10%)
  matrix products  43.8 us (9%)
  starting transfers between devices  10.8 us (2%)
    ppermute x2, waiting for transfers between devices, passed_along(): return lax.ppermute(array, axis, pairs)  78 us
    psum x1, blocking collectives, on_device(): sum_first, sum_second = lax.psum(group_sums(conv), 'rows')  72 us
    all_to_all x1, blocking collectives, on_device(): lax.all_to_all(banded, 'rows', split_axis=2, concat_axis=1, tiled=True)  68.1 us
    conv_general_dilated x6, local copies, waits for them, and re-layouts, conv_tap(): lax.conv_general_dilated(source, kernel, (2, 2), ((0, 0), (1, 1)), dimens...  49.7 us
    conv_general_dilated x3, matrix products, conv_tap(): lax.conv_general_dilated(source, kernel, (2, 2), ((0, 0), (1, 1)), dimens...  43.8 us
    conv_general_dilated x3, other arithmetic, conv_tap(): lax.conv_general_dilated(source, kernel, (2, 2), ((0, 0), (1, 1)), dimens...  25 us
    concatenate x2, local copies, waits for them, and re-layouts, on_device(): extended = jnp.concatenate([row_above, frames], axis=1)  21.8 us
    mul x2, local copies, waits for them, and re-layouts, on_device(): history[tap_index:tap_index + frame_count] * keep_mask[:, None, None, None]  17.1 us
  transfers between devices with their start and end apart: 2, of which 2 were waited for; matrix products, arithmetic and copies ran while one was open for 10% of the time, Pallas kernels for 0%

commit v1 on v0

v1 whole, which is shorter than its diff:
```python
import functools

import jax
import jax.numpy as jnp
from jax import lax
from jax.experimental import pallas as pl
from jax.experimental.pallas import tpu as pltpu
from jax.sharding import PartitionSpec as P

GROUPS = 32
EPS = 1e-05
MESH = pl.DeviceIdType.MESH
MIB = 2**20
FR = 4
BAND = 8
WIDTH = 1280
WO = 640
CI = 128
CO = 256
COLS = 20
PEERS = 32
TILE = 320
LEAD = 8


def repeat(count, body):
    lax.fori_loop(0, count, lambda u, c: (body(u), c)[1], 0)


def conv_kernel(
    clips, frames, weight, got, got_sums,
    rows_in, taps_in, stage, send, part_send, part_got, sums, sums_send,
    load_sem, halo_s, halo_r, part_s, part_r, out_s, out_r, sum_s, sum_r, own_sem,
):
    tm = lax.axis_index("tm")
    me = lax.axis_index("rows")
    tm_count = lax.axis_size("tm")
    tm_next = lax.rem(tm + 1, tm_count)
    tm_last = lax.rem(tm + tm_count - 1, tm_count)
    below = lax.rem(me + 1, PEERS)

    def peer(d):
        return lax.rem(me + 1 + d, PEERS)

    def load(f, part):
        first, count = ((3, 5), (0, 3))[part]
        return pltpu.make_async_copy(
            frames.at[f, pl.ds(first, count)],
            rows_in.at[f, pl.ds(first + 1, count)],
            load_sem.at[f, part],
        )

    for part in range(2):
        for f in (2, 0, 1, 3):
            load(f, part).start()

    barrier = pltpu.get_barrier_semaphore()
    repeat(
        PEERS - 1,
        lambda d: pl.semaphore_signal(barrier, inc=1, device_id=(tm, peer(d)), device_id_type=MESH),
    )
    for other in (tm_next, tm_last):
        pl.semaphore_signal(barrier, inc=1, device_id=(other, me), device_id_type=MESH)

    stage[0:LEAD] = jnp.zeros((LEAD, CI), jnp.float32)
    sums[...] = jnp.zeros(sums.shape, jnp.float32)

    above = jnp.where(me > 0, 1.0, 0.0).astype(jnp.float32)

    def split(f, first, count):
        def body(u):
            r = first + u
            row = rows_in[f, r].astype(jnp.float32)
            stage[LEAD : LEAD + WIDTH] = row if first else row * above
            for b in range(3):
                taps_in[f, r, :, b * CI : (b + 1) * CI] = stage[
                    pl.ds(LEAD - 1 + b, WO, stride=2), :
                ].astype(jnp.bfloat16)

        repeat(count, body)

    load(2, 0).wait()
    split(2, 4, 5)

    pl.semaphore_wait(barrier, PEERS + 1)

    def halo(f):
        return pltpu.make_async_remote_copy(
            frames.at[f, BAND - 1],
            rows_in.at[f, 0],
            halo_s.at[f],
            halo_r.at[f],
            device_id=(tm, below),
            device_id_type=MESH,
        )

    for f in (2, 3, 0, 1):
        halo(f).start()

    start = tm * FR

    def mask(target, source):
        inside = jnp.logical_or(tm < tm_count - 1, target < FR)
        last = tm_count * FR
        same = clips[lax.rem(start + target, last)] == clips[lax.rem(start + source, last)]
        return jnp.where(jnp.logical_and(inside, same), 1.0, 0.0).astype(jnp.float32)

    def dots(terms, row, col):
        total = None
        for f, k, m in terms:
            left = jnp.concatenate(
                [taps_in[f, 2 * row + a, pl.ds(col, TILE), :] for a in range(3)], axis=1
            )
            term = jnp.dot(left, weight[k], preferred_element_type=jnp.float32)
            if m is not None:
                term = term * m
            total = term if total is None else total + term
        return total

    def part_copy(g, n):
        return pltpu.make_async_remote_copy(
            part_send.at[g, n],
            part_got.at[g, n],
            part_s.at[g, n],
            part_r.at[g, n],
            device_id=(tm_next, me),
            device_id_type=MESH,
        )

    def partial_sums(g, n):
        if n == 0:
            terms = [(2, 0, mask(4, 2)), (3, 1, mask(4, 3))]
        else:
            terms = [(3, 0, mask(5, 3))]

        def body(u):
            r, q = u // 2, lax.rem(u, 2)
            col = pl.multiple_of(q * TILE, TILE)
            value = dots(terms, 2 - 2 * g + r, col)
            part_send[g, n, r, pl.ds(col, TILE), :] = value.astype(jnp.bfloat16)

        repeat(4, body)
        part_copy(g, n).start()

    def out_copy(t, g, to):
        return pltpu.make_async_remote_copy(
            send.at[t, g, to],
            got.at[t, g, me],
            out_s.at[t, g],
            out_r.at[t, g],
            device_id=(tm, to),
            device_id_type=MESH,
        )

    def own_copy(t, g):
        return pltpu.make_async_copy(send.at[t, g, me], got.at[t, g, me], own_sem.at[t, g])

    def outputs(t, g):
        terms = [
            (t - 2 + k, k, None if k == 2 else mask(t, t - 2 + k)) for k in range(3) if t - 2 + k >= 0
        ]

        def body(q):
            col = pl.multiple_of(q * TILE, TILE)
            row = 2 - 2 * g
            upper = dots(terms, row, col)
            lower = dots(terms, row + 1, col)
            if t < 2:
                upper = upper + part_got[g, t, 0, pl.ds(col, TILE), :].astype(jnp.float32)
                lower = lower + part_got[g, t, 1, pl.ds(col, TILE), :].astype(jnp.float32)
            by8 = (TILE // 8, 8, CO)
            sums[t, 0] += jnp.sum((upper + lower).reshape(by8), axis=0)
            sums[t, 1] += jnp.sum((upper * upper + lower * lower).reshape(by8), axis=0)
            pairs = TILE // (2 * COLS)
            upper = upper.reshape(pairs, 2 * COLS, CO)
            lower = lower.reshape(pairs, 2 * COLS, CO)
            even = jnp.concatenate([upper[:, :COLS], lower[:, :COLS]], axis=1)
            odd = jnp.concatenate([upper[:, COLS:], lower[:, COLS:]], axis=1)
            for j in range(pairs):
                to = q * (2 * pairs) + 2 * j
                send[t, g, to] = even[j].astype(jnp.bfloat16)
                send[t, g, to + 1] = odd[j].astype(jnp.bfloat16)

        repeat(2, body)
        repeat(PEERS - 1, lambda d: out_copy(t, g, peer(d)).start())
        own_copy(t, g).start()

    def sum_copy(t, to):
        return pltpu.make_async_remote_copy(
            sums_send.at[t],
            got_sums.at[t, me],
            sum_s.at[t],
            sum_r.at[t],
            device_id=(tm, to),
            device_id_type=MESH,
        )

    def own_sums(t):
        return pltpu.make_async_copy(sums_send.at[t], got_sums.at[t, me], own_sem.at[t, 2])

    def group_sums(t):
        sums_send[t] = jnp.sum(sums[t], axis=1)
        repeat(PEERS - 1, lambda d: sum_copy(t, peer(d)).start())
        own_sums(t).start()

    for f in (0, 1):
        load(f, 0).wait()
        split(f, 4, 5)
    outputs(2, 0)
    load(3, 0).wait()
    split(3, 4, 5)
    partial_sums(0, 0)
    partial_sums(0, 1)
    outputs(3, 0)
    for f in (2, 3, 0, 1):
        load(f, 1).wait()
        split(f, 1, 3)
        halo(f).wait_recv()
        split(f, 0, 1)
        if f == 3:
            partial_sums(1, 0)
            partial_sums(1, 1)
    for t in (2, 3):
        outputs(t, 1)
        group_sums(t)
    for g in range(2):
        for t in range(2):
            part_copy(g, t).wait_recv()
            outputs(t, g)
            if g == 1:
                group_sums(t)

    for f in range(FR):
        halo(f).wait_send()
    for g in range(2):
        for t in range(2):
            part_copy(g, t).wait_send()
    for t in (2, 3, 0, 1):
        for g in range(2):
            own_copy(t, g).wait()
            every = pltpu.make_async_remote_copy(
                send.at[t, g, pl.ds(0, PEERS - 1)],
                got.at[t, g, pl.ds(0, PEERS - 1)],
                out_s.at[t, g],
                out_r.at[t, g],
                device_id=(tm, below),
                device_id_type=MESH,
            )
            every.wait()
        own_sums(t).wait()
        sent = pltpu.make_async_remote_copy(
            got_sums.at[t, pl.ds(0, PEERS - 1)],
            got_sums.at[t, pl.ds(0, PEERS - 1)],
            sum_s.at[t],
            sum_r.at[t],
            device_id=(tm, below),
            device_id_type=MESH,
        )
        sent.wait()


def conv_call(clips, frames, weight):
    dma = pltpu.SemaphoreType.DMA
    return pl.pallas_call(
        conv_kernel,
        out_shape=[
            jax.ShapeDtypeStruct((FR, 2, PEERS, 2 * COLS, CO), jnp.bfloat16),
            jax.ShapeDtypeStruct((FR, PEERS, 2, CO), jnp.float32),
        ],
        in_specs=[
            pl.BlockSpec(memory_space=pltpu.SMEM),
            pl.BlockSpec(memory_space=pl.ANY),
            pl.BlockSpec(memory_space=pltpu.VMEM),
        ],
        out_specs=[pl.BlockSpec(memory_space=pl.ANY)] * 2,
        scratch_shapes=[
            pltpu.VMEM((FR, BAND + 1, WIDTH, CI), jnp.bfloat16),
            pltpu.VMEM((FR, BAND + 1, WO, 3 * CI), jnp.bfloat16),
            pltpu.VMEM((LEAD + WIDTH + 8, CI), jnp.float32),
            pltpu.VMEM((FR, 2, PEERS, 2 * COLS, CO), jnp.bfloat16),
            pltpu.VMEM((2, 2, 2, WO, CO), jnp.bfloat16),
            pltpu.VMEM((2, 2, 2, WO, CO), jnp.bfloat16),
            pltpu.VMEM((FR, 2, 8, CO), jnp.float32),
            pltpu.VMEM((FR, 2, CO), jnp.float32),
            dma((FR, 2)), dma((FR,)), dma((FR,)), dma((2, 2)), dma((2, 2)),
            dma((FR, 2)), dma((FR, 2)), dma((FR,)), dma((FR,)), dma((FR, 3)),
        ],
        compiler_params=pltpu.CompilerParams(
            collective_id=0, has_side_effects=True, vmem_limit_bytes=58 * MIB
        ),
        name="conv",
    )(clips, frames, weight)


PITCH = 136


def group_totals(sums):
    lane = lax.broadcasted_iota(jnp.int32, sums.shape, 1)
    for by in (1, 2, 4):
        up, down = pltpu.roll(sums, CO - by, 1), pltpu.roll(sums, by, 1)
        sums = sums + jnp.where(lax.rem(lane // by, 2) == 0, up, down)
    return sums


def norm_kernel(entries, got, got_sums, gain, bias, latent, columns):
    total = jnp.sum(got_sums[0], axis=0)
    total = group_totals(jnp.concatenate([total, jnp.zeros((6, CO), jnp.float32)], axis=0))
    mean = total[0:1] / entries
    variance = total[1:2] / entries - mean * mean
    scale = lax.rsqrt(variance + EPS) * gain[...]
    shift = bias[...]
    for s in range(PEERS):
        for g in range(2):
            value = got[0, g, s].astype(jnp.float32)
            half = ((value - mean) * scale + shift) * 0.5
            value = half * jnp.tanh(half) + half
            for r in range(2):
                for h in range(2):
                    columns[h, pl.ds(4 * s + 2 - 2 * g + r, COLS, stride=PITCH), :] = value[
                        r * COLS : (r + 1) * COLS, h * 128 : (h + 1) * 128
                    ]
    for j in range(COLS):
        for h in range(2):
            latent[0, j, :, h * 128 : (h + 1) * 128] = columns[
                h, pl.ds(j * PITCH, 4 * PEERS), :
            ].astype(jnp.bfloat16)


def norm_call(got, got_sums, gain, bias):
    latent = pl.pallas_call(
        functools.partial(norm_kernel, float(PEERS * 4 * WO * (CO // GROUPS))),
        grid=(FR,),
        out_shape=jax.ShapeDtypeStruct((FR, COLS, PEERS * 4, CO), jnp.bfloat16),
        in_specs=[
            pl.BlockSpec((1, 2, PEERS, 2 * COLS, CO), lambda t: (t, 0, 0, 0, 0)),
            pl.BlockSpec((1, PEERS, 2, CO), lambda t: (t, 0, 0, 0)),
            pl.BlockSpec((1, CO), lambda t: (0, 0)),
            pl.BlockSpec((1, CO), lambda t: (0, 0)),
        ],
        out_specs=pl.BlockSpec((1, COLS, PEERS * 4, CO), lambda t: (t, 0, 0, 0)),
        scratch_shapes=[pltpu.VMEM((2, COLS * PITCH, 128), jnp.float32)],
        compiler_params=pltpu.CompilerParams(vmem_limit_bytes=60 * MIB),
        name="norm",
    )(got, got_sums, gain, bias)
    return latent.transpose(0, 2, 1, 3)


def on_device(frames, clip_ids, conv_weight, norm_gain, norm_bias):
    weight = conv_weight.reshape(3, 9 * CI, CO)
    got, got_sums = conv_call(clip_ids, frames, weight)
    return norm_call(got, got_sums, norm_gain.reshape(1, CO), norm_bias.reshape(1, CO))


def solution(mesh):
    in_specs = (P("tm", "rows", None, None), P(), P(), P(), P())
    out_specs = P("tm", None, "rows", None)
    return jax.shard_map(
        on_device, mesh=mesh, in_specs=in_specs, out_specs=out_specs, check_vma=False
    )
```

time: 475 us -> 103 us (0.22)
  local copies, waits for them, and re-layouts: 147 us -> 0 us
  blocking collectives: 140 us -> 0 us
  Pallas kernels: 0 us -> 102 us
  waiting for transfers between devices: 78 us -> 0 us
  other arithmetic: 49.7 us -> 0 us
  matrix products: 43.8 us -> 0 us
  starting transfers between devices: 10.8 us -> 0 us
    pallas_call x0 -> x2, Pallas kernels: none -> 102 us  [the longest x1 93.3 us: conv_call(): pl.pallas_call(conv_kernel, out_shape=[jax.ShapeDtypeStruct((FR, 2, PEERS...]
    ppermute x2 -> x0, waiting for transfers between devices: 78 us -> none  [passed_along(): return lax.ppermute(array, axis, pairs)]
    psum x1 -> x0, blocking collectives: 72 us -> none  [on_device(): sum_first, sum_second = lax.psum(group_sums(conv), 'rows')]
    all_to_all x1 -> x0, blocking collectives: 68.1 us -> none  [on_device(): lax.all_to_all(banded, 'rows', split_axis=2, concat_axis=1, tiled=True)]
    conv_general_dilated x6 -> x0, local copies, waits for them, and re-layouts: 49.7 us -> none  [conv_tap(): lax.conv_general_dilated(source, kernel, (2, 2), ((0, 0), (1, 1)), dimens...]
    conv_general_dilated x3 -> x0, matrix products: 43.8 us -> none  [conv_tap(): lax.conv_general_dilated(source, kernel, (2, 2), ((0, 0), (1, 1)), dimens...]
    mul x6 -> x0, local copies, waits for them, and re-layouts: 35.3 us -> none  [the longest x2 17.1 us: on_device(): history[tap_index:tap_index + frame_count] * keep_mask[:, None, None, None]]
    conv_general_dilated x3 -> x0, other arithmetic: 25 us -> none  [conv_tap(): lax.conv_general_dilated(source, kernel, (2, 2), ((0, 0), (1, 1)), dimens...]
  transfers between devices with their start and end apart: 2 -> 0, of which waited for: 2 -> 0; matrix products, arithmetic and copies ran while one was open for 10% -> 0% of each run, Pallas kernels for 0% -> 0%
where the time goes in v1:
time: 103 us; the launch traced here: 102 us
  Pallas kernels  102 us (99%)
    pallas_call x1, Pallas kernels, conv_call(): pl.pallas_call(conv_kernel, out_shape=[jax.ShapeDtypeStruct((FR, 2, PEERS...  93.3 us
    pallas_call x1, Pallas kernels, norm_call(): pl.pallas_call(functools.partial(norm_kernel, float(PEERS * 4 * WO * (CO...  8.23 us

profile of v1, /device:TPU:1, one launch (start us, length us, event | category | flops | bytes accessed | tf_op | source)
XLA Modules:
  0.0 101.5 jit_solution(17476513151286366019)
XLA Ops:
  0.0 93.3 %conv.1 = (bf16[4,2,32,40,256]{4,3,2,1,0:T(8,128)(2,1)}, f32[4,32,2,256]{3,2,1,0:T(2,128)}) custom-call(s32[16]{0:T(128)} %clips.1, bf16[4,8,1280,128]{3,2,1,0:T(8,128)(2,1)} %frames.1, bf16[3,1152,256]{2,1,0:T(8,128)(2,1)} %bitcast.4), custom_call_target="tpu_custom_call" | custom-call | tf_op jit(solution)/shard_map/conv/pallas_call | solution.py:264
  93.3 8.2 %norm.1 = bf16[4,20,128,256]{3,2,1,0:T(8,128)(2,1)} custom-call(bf16[4,2,32,40,256]{4,3,2,1,0:T(8,128)(2,1)} %get-tuple-element.7.got, f32[4,32,2,256]{3,2,1,0:T(2,128)} %get-tuple-element.8.got_sums, f32[1,256]{1,0:T(1,128)} %bitcast.5, f32[1,256]{1,0:T(1,128)} %bitcast.6), custom_call_target="tpu_custom_call" | custom-call | tf_op jit(solution)/shard_map/norm/pallas_call | solution.py:331

commit v2 on v1

v2 whole, which is shorter than its diff:
```python
import functools

import jax
import jax.numpy as jnp
from jax import lax
from jax.experimental import pallas as pl
from jax.experimental.pallas import tpu as pltpu
from jax.sharding import PartitionSpec as P

GROUPS = 32
EPS = 1e-05
MESH = pl.DeviceIdType.MESH
MIB = 2**20
FR = 4
BAND = 8
WIDTH = 1280
WO = 640
CI = 128
CO = 256
COLS = 20
PEERS = 32
TILE = 320
PIECE = 160
PIECES = WIDTH // PIECE
RELAYED = ((2, 0), (3, 0))


def repeat(count, body):
    lax.fori_loop(0, count, lambda u, c: (body(u), c)[1], 0)


PITCH = 136


def group_totals(sums):
    lane = lax.broadcasted_iota(jnp.int32, sums.shape, 1)
    for by in (1, 2, 4):
        up, down = pltpu.roll(sums, CO - by, 1), pltpu.roll(sums, by, 1)
        sums = sums + jnp.where(lax.rem(lane // by, 2) == 0, up, down)
    return sums


def moments(sums, gain, entries):
    total = jnp.sum(sums, axis=0)
    total = group_totals(jnp.concatenate([total, jnp.zeros((6, CO), jnp.float32)], axis=0))
    mean = total[0:1] / entries
    variance = total[1:2] / entries - mean * mean
    return mean, lax.rsqrt(variance + EPS) * gain


def normalize(frame, sums, gain, bias, latent, columns, entries):
    mean, scale = moments(sums[...], gain[...], entries)
    scale = scale * 0.5
    shift = bias[...] * 0.5
    for s in range(PEERS):
        for g in range(2):
            half = (frame[g, s].astype(jnp.float32) - mean) * scale + shift
            value = half * jnp.tanh(half) + half
            for r in range(2):
                for h in range(2):
                    columns[h, pl.ds(4 * s + 2 - 2 * g + r, COLS, stride=PITCH), :] = value[
                        r * COLS : (r + 1) * COLS, h * 128 : (h + 1) * 128
                    ]
    for j in range(COLS):
        for h in range(2):
            latent[j, :, h * 128 : (h + 1) * 128] = columns[
                h, pl.ds(j * PITCH, 4 * PEERS), :
            ].astype(jnp.bfloat16)


def conv_kernel(
    entries, clips, frames, weight_in, gain, bias, got, got_sums, done,
    rows_in, taps_in, weight, send, part_send, part_got, sums, sums_send,
    frame, frame_sums, frame_out, columns,
    load_sem, halo_s, halo_r, part_s, part_r, out_s, out_r, sum_s, sum_r, own_sem, norm_sem, relay, relay_s, relay_r, forward_s,
):
    tm = lax.axis_index("tm")
    me = lax.axis_index("rows")
    tm_count = lax.axis_size("tm")
    tm_next = lax.rem(tm + 1, tm_count)
    tm_last = lax.rem(tm + tm_count - 1, tm_count)
    below = lax.rem(me + 1, PEERS)

    def load(f, part):
        first, count = ((3, 5), (0, 3))[part]
        return pltpu.make_async_copy(
            frames.at[f, pl.ds(first, count)],
            rows_in.at[f, pl.ds(first + 1, count)],
            load_sem.at[f, part],
        )

    load_weight = pltpu.make_async_copy(weight_in, weight, load_sem.at[FR, 0])
    load(2, 0).start()
    load(3, 0).start()
    load_weight.start()
    load(0, 0).start()
    load(1, 0).start()
    for f in (2, 3, 0, 1):
        load(f, 1).start()

    barrier = pltpu.get_barrier_semaphore()

    def greet(d):
        to = lax.rem(me + 1 + d, PEERS)
        pl.semaphore_signal(barrier, inc=1, device_id=(tm, to), device_id_type=MESH)

    repeat(PEERS - 1, greet)
    for other in (tm_next, tm_last):
        pl.semaphore_signal(barrier, inc=1, device_id=(other, me), device_id_type=MESH)

    sums[...] = jnp.zeros(sums.shape, jnp.float32)
    above = jnp.where(me > 0, 1.0, 0.0).astype(jnp.bfloat16)

    def split(f, first, count):
        def body(u):
            r = first + u
            row = rows_in[f, r]
            pairs = (row if first else row * above).reshape(WO, 2 * CI)
            taps_in[f, r, :, CI:] = pairs
            before = jnp.zeros((1, CI), jnp.bfloat16)
            taps_in[f, r, :, :CI] = jnp.concatenate([before, pairs[:-1, CI:]], axis=0)

        repeat(count, body)

    start = tm * FR

    def mask(target, source):
        inside = jnp.logical_or(tm < tm_count - 1, target < FR)
        last = tm_count * FR
        same = clips[lax.rem(start + target, last)] == clips[lax.rem(start + source, last)]
        return jnp.where(jnp.logical_and(inside, same), 1.0, 0.0).astype(jnp.float32)

    def dots(terms, row, col):
        total = None
        for f, k, m in terms:
            left = jnp.concatenate(
                [taps_in[f, 2 * row + a, pl.ds(col, TILE), :] for a in range(3)], axis=1
            )
            term = jnp.dot(left, weight[k], preferred_element_type=jnp.float32)
            if m is not None:
                term = term * m
            total = term if total is None else total + term
        return total

    def halo(f):
        return pltpu.make_async_remote_copy(
            frames.at[f, BAND - 1],
            rows_in.at[f, 0],
            halo_s.at[f],
            halo_r.at[f],
            device_id=(tm, below),
            device_id_type=MESH,
        )

    def halo_pieces(first, count):
        def body(u):
            i = first + u
            f = lax.rem(i // PIECES * 2, 4) + i // (2 * PIECES)
            at = pl.ds(pl.multiple_of(lax.rem(i, PIECES) * PIECE, PIECE), PIECE)
            pltpu.make_async_remote_copy(
                frames.at[f, BAND - 1, at],
                rows_in.at[f, 0, at],
                halo_s.at[f],
                halo_r.at[f],
                device_id=(tm, below),
                device_id_type=MESH,
            ).start()

        repeat(count, body)

    def part_copy(n, row):
        return pltpu.make_async_remote_copy(
            part_send.at[n, row],
            part_got.at[n, row],
            part_s.at[n, row],
            part_r.at[n, row],
            device_id=(tm_next, me),
            device_id_type=MESH,
        )

    def partial_sums(n, row):
        if n == 0:
            terms = [(2, 0, mask(4, 2)), (3, 1, mask(4, 3))]
        else:
            terms = [(3, 0, mask(5, 3))]

        def body(q):
            col = pl.multiple_of(q * TILE, TILE)
            part_send[n, row, pl.ds(col, TILE), :] = dots(terms, row, col).astype(jnp.bfloat16)

        repeat(2, body)
        part_copy(n, row).start()

    def out_copy(t, g, to):
        return pltpu.make_async_remote_copy(
            send.at[t, g, to],
            got.at[t, g, me],
            out_s.at[t, g],
            out_r.at[t, g],
            device_id=(tm, to),
            device_id_type=MESH,
        )

    y, z, core = me // 8, lax.rem(me // 2, 4), lax.rem(me, 2)
    z_less, z_more, z_two = lax.rem(z + 3, 4), lax.rem(z + 1, 4), lax.rem(z + 2, 4)

    def relay_copy(n, d):
        t, g = RELAYED[n]
        to = lax.rem(y + d // 2, 4) * 8 + z_two * 2 + lax.rem(core + d, 2)
        return pltpu.make_async_remote_copy(
            send.at[t, g, to],
            relay.at[n, d],
            relay_s.at[n],
            relay_r.at[n],
            device_id=(tm, y * 8 + z_less * 2 + core),
            device_id_type=MESH,
        )

    def forward(n):
        t, g = RELAYED[n]
        source = y * 8 + z_more * 2 + core
        relay_all(n).wait_recv()

        def body(d):
            to = lax.rem(y + d // 2, 4) * 8 + z_less * 2 + lax.rem(core + d, 2)
            pltpu.make_async_remote_copy(
                relay.at[n, d],
                got.at[t, g, source],
                forward_s.at[n],
                out_r.at[t, g],
                device_id=(tm, to),
                device_id_type=MESH,
            ).start()

        repeat(8, body)

    def relay_all(n):
        return pltpu.make_async_remote_copy(
            relay.at[n], relay.at[n], relay_s.at[n], relay_r.at[n],
            device_id=(tm, below), device_id_type=MESH,
        )

    def forward_all(n):
        return pltpu.make_async_remote_copy(
            relay.at[n], relay.at[n], forward_s.at[n], relay_r.at[n],
            device_id=(tm, below), device_id_type=MESH,
        )

    def own_copy(t, g):
        return pltpu.make_async_copy(send.at[t, g, me], got.at[t, g, me], own_sem.at[t, g])

    def outputs(t, g):
        terms = [
            (t - 2 + k, k, None if k == 2 else mask(t, t - 2 + k)) for k in range(3) if t - 2 + k >= 0
        ]
        row = 2 - 2 * g
        pairs = TILE // (2 * COLS)

        def body(u):
            q = lax.rem(u + z, 2)
            col = pl.multiple_of(q * TILE, TILE)
            upper = dots(terms, row, col)
            lower = dots(terms, row + 1, col)
            if t < 2:
                upper = upper + part_got[t, row, pl.ds(col, TILE), :].astype(jnp.float32)
                lower = lower + part_got[t, row + 1, pl.ds(col, TILE), :].astype(jnp.float32)
            by8 = (TILE // 8, 8, CO)
            sums[t, 0] += jnp.sum((upper + lower).reshape(by8), axis=0)
            sums[t, 1] += jnp.sum((upper * upper + lower * lower).reshape(by8), axis=0)
            upper = upper.reshape(pairs, 2 * COLS, CO)
            lower = lower.reshape(pairs, 2 * COLS, CO)
            even = jnp.concatenate([upper[:, :COLS], lower[:, :COLS]], axis=1)
            odd = jnp.concatenate([upper[:, COLS:], lower[:, COLS:]], axis=1)
            for j in range(pairs):
                to = q * (2 * pairs) + 2 * j
                send[t, g, to] = even[j].astype(jnp.bfloat16)
                send[t, g, to + 1] = odd[j].astype(jnp.bfloat16)

            if (t, g) in ((2, 0), (3, 0)):
                halo_pieces(12 + 10 * (t - 2) + 5 * u, 5)

            def push(d):
                to = q * (2 * pairs) + lax.rem(me + 1 + 3 * d, 2 * pairs)
                direct = to != me
                if (t, g) in RELAYED:
                    direct = jnp.logical_and(direct, lax.rem(to // 2, 4) != z_two)

                @pl.when(direct)
                def _():
                    out_copy(t, g, to).start()

            repeat(2 * pairs, push)

        repeat(2, body)
        own_copy(t, g).start()
        if (t, g) in RELAYED:
            repeat(8, lambda d: relay_copy(RELAYED.index((t, g)), d).start())

    def sum_copy(t, to):
        return pltpu.make_async_remote_copy(
            sums_send.at[t],
            got_sums.at[t, me],
            sum_s.at[t],
            sum_r.at[t],
            device_id=(tm, to),
            device_id_type=MESH,
        )

    def own_sums(t):
        return pltpu.make_async_copy(sums_send.at[t], got_sums.at[t, me], own_sem.at[t, 2])

    def group_sums(t):
        sums_send[t] = jnp.sum(sums[t], axis=1)
        repeat(PEERS - 1, lambda d: sum_copy(t, lax.rem(me + 1 + d, PEERS)).start())
        own_sums(t).start()

    pl.semaphore_wait(barrier, PEERS + 1)
    halo_pieces(0, 12)
    for f in (2, 3):
        load(f, 0).wait()
        split(f, 4, 5)
    load_weight.wait()
    partial_sums(0, 2)
    for f in (0, 1):
        load(f, 0).wait()
        split(f, 4, 5)
    outputs(2, 0)
    partial_sums(0, 3)
    outputs(3, 0)
    partial_sums(1, 2)
    partial_sums(1, 3)
    for f in (2, 3):
        load(f, 1).wait()
        split(f, 1, 3)
    partial_sums(0, 1)
    partial_sums(1, 1)
    for f in (0, 1):
        load(f, 1).wait()
        split(f, 1, 3)
    for f in (0, 2, 1, 3):
        halo(f).wait_recv()
    for n in range(len(RELAYED)):
        forward(n)
    for f in (0, 1, 2, 3):
        split(f, 0, 1)
    outputs(2, 1)
    group_sums(2)
    partial_sums(0, 0)
    outputs(3, 1)
    group_sums(3)
    partial_sums(1, 0)
    for g in range(2):
        for t in range(2):
            for r in range(2):
                part_copy(t, 2 - 2 * g + r).wait_recv()
            outputs(t, g)
            if g == 1:
                group_sums(t)

    def out_all(t, g, count):
        return pltpu.make_async_remote_copy(
            send.at[t, g, pl.ds(0, count)],
            got.at[t, g, pl.ds(0, count)],
            out_s.at[t, g],
            out_r.at[t, g],
            device_id=(tm, below),
            device_id_type=MESH,
        )

    def arrived(t):
        for g in range(2):
            own_copy(t, g).wait()
            direct = PEERS - 1 - (8 if (t, g) in RELAYED else 0)
            out_all(t, g, direct).wait_send()
            out_all(t, g, PEERS - 1).wait_recv()
        own_sums(t).wait()
        sent = pltpu.make_async_remote_copy(
            got_sums.at[t, pl.ds(0, PEERS - 1)],
            got_sums.at[t, pl.ds(0, PEERS - 1)],
            sum_s.at[t],
            sum_r.at[t],
            device_id=(tm, below),
            device_id_type=MESH,
        )
        sent.wait()

    for n, t in enumerate((2, 3)):
        arrived(t)
        fetch = pltpu.make_async_copy(got.at[t], frame, norm_sem.at[0])
        fetch_sums = pltpu.make_async_copy(got_sums.at[t], frame_sums, norm_sem.at[1])
        fetch.start()
        fetch_sums.start()
        fetch.wait()
        fetch_sums.wait()
        normalize(frame, frame_sums, gain, bias, frame_out.at[n], columns, entries)
        pltpu.make_async_copy(frame_out.at[n], done.at[n], norm_sem.at[2 + n]).start()

    for f in range(FR):
        halo(f).wait_send()
    for n in range(2):
        for row in range(4):
            part_copy(n, row).wait_send()
    for n in range(2):
        pltpu.make_async_copy(frame_out.at[n], done.at[n], norm_sem.at[2 + n]).wait()
    for n in range(len(RELAYED)):
        relay_all(n).wait_send()
        forward_all(n).wait_send()
    arrived(0)
    arrived(1)


def conv_call(clips, frames, weight, gain, bias, entries):
    dma = pltpu.SemaphoreType.DMA
    anywhere = pl.BlockSpec(memory_space=pl.ANY)
    return pl.pallas_call(
        functools.partial(conv_kernel, entries),
        out_shape=[
            jax.ShapeDtypeStruct((FR, 2, PEERS, 2 * COLS, CO), jnp.bfloat16),
            jax.ShapeDtypeStruct((FR, PEERS, 2, CO), jnp.float32),
            jax.ShapeDtypeStruct((2, COLS, PEERS * 4, CO), jnp.bfloat16),
        ],
        in_specs=[
            pl.BlockSpec(memory_space=pltpu.SMEM),
            anywhere,
            anywhere,
            pl.BlockSpec(memory_space=pltpu.VMEM),
            pl.BlockSpec(memory_space=pltpu.VMEM),
        ],
        out_specs=[anywhere] * 3,
        scratch_shapes=[
            pltpu.VMEM((FR, BAND + 1, WIDTH, CI), jnp.bfloat16),
            pltpu.VMEM((FR, BAND + 1, WO, 3 * CI), jnp.bfloat16),
            pltpu.VMEM((3, 9 * CI, CO), jnp.bfloat16),
            pltpu.VMEM((FR, 2, PEERS, 2 * COLS, CO), jnp.bfloat16),
            pltpu.VMEM((2, 4, WO, CO), jnp.bfloat16),
            pltpu.VMEM((2, 4, WO, CO), jnp.bfloat16),
            pltpu.VMEM((FR, 2, 8, CO), jnp.float32),
            pltpu.VMEM((FR, 2, CO), jnp.float32),
            pltpu.VMEM((2, PEERS, 2 * COLS, CO), jnp.bfloat16),
            pltpu.VMEM((PEERS, 2, CO), jnp.float32),
            pltpu.VMEM((2, COLS, PEERS * 4, CO), jnp.bfloat16),
            pltpu.VMEM((2, COLS * PITCH, 128), jnp.float32),
            dma((FR + 1, 2)), dma((FR,)), dma((FR,)), dma((2, 4)), dma((2, 4)),
            dma((FR, 2)), dma((FR, 2)), dma((FR,)), dma((FR,)), dma((FR, 3)), dma((4,)),
            pltpu.VMEM((len(RELAYED), 8, 2 * COLS, CO), jnp.bfloat16),
            dma((len(RELAYED),)), dma((len(RELAYED),)), dma((len(RELAYED),)),
        ],
        compiler_params=pltpu.CompilerParams(
            collective_id=0, has_side_effects=True, vmem_limit_bytes=60 * MIB
        ),
        name="conv",
    )(clips, frames, weight, gain, bias)


def last_kernel(
    entries, got, got_sums, gain, bias, done, latent,
    frame, frame_sums, frame_out, columns, kept, got_sem, sum_sem, out_sem, in_sem, back_sem,
):
    def fetch(t):
        return pltpu.make_async_copy(got.at[t], frame.at[t], got_sem.at[t])

    def fetch_sums(t):
        return pltpu.make_async_copy(got_sums.at[t], frame_sums.at[t], sum_sem.at[t])

    def into(n):
        return pltpu.make_async_copy(done.at[n], kept.at[n], in_sem.at[n])

    def back(n):
        return pltpu.make_async_copy(kept.at[n], latent.at[2 + n], back_sem.at[n])

    def out(t):
        return pltpu.make_async_copy(frame_out.at[t], latent.at[t], out_sem.at[t])

    for t in range(2):
        fetch_sums(t).start()
        fetch(t).start()
    for n in range(2):
        into(n).start()
    for t in range(2):
        fetch_sums(t).wait()
        fetch(t).wait()
        normalize(frame.at[t], frame_sums.at[t], gain, bias, frame_out.at[t], columns, entries)
        out(t).start()
        into(t).wait()
        back(t).start()
    for t in range(2):
        out(t).wait()
        back(t).wait()


def last_call(got, got_sums, gain, bias, done, entries):
    anywhere = pl.BlockSpec(memory_space=pl.ANY)
    inside = pl.BlockSpec(memory_space=pltpu.VMEM)
    return pl.pallas_call(
        functools.partial(last_kernel, entries),
        out_shape=jax.ShapeDtypeStruct((FR, COLS, PEERS * 4, CO), jnp.bfloat16),
        in_specs=[anywhere, anywhere, inside, inside, anywhere],
        out_specs=anywhere,
        scratch_shapes=[
            pltpu.VMEM((2, 2, PEERS, 2 * COLS, CO), jnp.bfloat16),
            pltpu.VMEM((2, PEERS, 2, CO), jnp.float32),
            pltpu.VMEM((2, COLS, PEERS * 4, CO), jnp.bfloat16),
            pltpu.VMEM((2, COLS * PITCH, 128), jnp.float32),
            pltpu.VMEM((2, COLS, PEERS * 4, CO), jnp.bfloat16),
            pltpu.SemaphoreType.DMA((2,)),
            pltpu.SemaphoreType.DMA((2,)),
            pltpu.SemaphoreType.DMA((2,)),
            pltpu.SemaphoreType.DMA((2,)),
            pltpu.SemaphoreType.DMA((2,)),
        ],
        compiler_params=pltpu.CompilerParams(vmem_limit_bytes=60 * MIB),
        name="last",
    )(got, got_sums, gain, bias, done)


def on_device(frames, clip_ids, conv_weight, norm_gain, norm_bias):
    weight = conv_weight.reshape(3, 9 * CI, CO)
    gain, bias = norm_gain.reshape(1, CO), norm_bias.reshape(1, CO)
    entries = float(PEERS * 4 * WO * (CO // GROUPS))
    got, got_sums, done = conv_call(clip_ids, frames, weight, gain, bias, entries)
    latent = last_call(got, got_sums, gain, bias, done, entries)
    return latent.transpose(0, 2, 1, 3)


def solution(mesh):
    in_specs = (P("tm", "rows", None, None), P(), P(), P(), P())
    out_specs = P("tm", None, "rows", None)
    return jax.shard_map(
        on_device, mesh=mesh, in_specs=in_specs, out_specs=out_specs, check_vma=False
    )
```

time: 103 us -> 92.8 us (0.901); the launches traced: 102 us -> 92.6 us
  Pallas kernels: 102 us -> 92.4 us
    pallas_call x2, Pallas kernels: 102 us -> 92.4 us  [the longest x1 86.4 us: conv_call(): pl.pallas_call(functools.partial(conv_kernel, entries), out_shape=[jax.Sh...]
where the time goes in v2:
time: 92.8 us; the launch traced here: 92.6 us
  Pallas kernels  92.4 us (100%)
    pallas_call x1, Pallas kernels, conv_call(): pl.pallas_call(functools.partial(conv_kernel, entries), out_shape=[jax.Sh...  86.4 us
    pallas_call x1, Pallas kernels, last_call(): pl.pallas_call(functools.partial(last_kernel, entries), out_shape=jax.Sha...  6.06 us

profile of v2, /device:TPU:1, one launch (start us, length us, event | category | flops | bytes accessed | tf_op | source)
XLA Modules:
  0.0 92.6 jit_solution(17330270214587618342)
XLA Ops:
  0.0 86.4 %conv.1 = (bf16[4,2,32,40,256]{4,3,2,1,0:T(8,128)(2,1)}, f32[4,32,2,256]{3,2,1,0:T(2,128)}, bf16[2,20,128,256]{3,2,1,0:T(8,128)(2,1)}) custom-call(s32[16]{0:T(128)} %clips.1, bf16[4,8,1280,128]{3,2,1,0:T(8,128)(2,1)} %frames.1, bf16[3,1152,256]{2,1,0:T(8,128)(2,1)} %bitcast.4, f32[1,256]{1,0:T(1,128)} %bitcast.5, f32[1,256]{1,0:T(1,128)} %bitcast.7), custom_call_target="tpu_custom_call" | custom-call | tf_op jit(solution)/shard_map/conv/pallas_call | solution.py:415
  86.4 6.1 %last.1 = bf16[4,20,128,256]{3,2,1,0:T(8,128)(2,1)} custom-call(bf16[4,2,32,40,256]{4,3,2,1,0:T(8,128)(2,1)} %get-tuple-element.8.got, f32[4,32,2,256]{3,2,1,0:T(2,128)} %get-tuple-element.9.got_sums, f32[1,256]{1,0:T(1,128)} %bitcast.6, f32[1,256]{1,0:T(1,128)} %bitcast.8, bf16[2,20,128,256]{3,2,1,0:T(8,128)(2,1)} %get-tuple-element.10.done), custom_call_target="tpu_custom_call" | custom-call | tf_op jit(solution)/shard_map/last/pallas_call | solution.py:494

commit v3 on v2

--- a/solution.py
+++ b/solution.py
@@ -257,7 +257,7 @@
         pairs = TILE // (2 * COLS)
 
         def body(u):
-            q = lax.rem(u + z, 2)
+            q = u
             col = pl.multiple_of(q * TILE, TILE)
             upper = dots(terms, row, col)
             lower = dots(terms, row + 1, col)
@@ -276,25 +276,23 @@
                 send[t, g, to] = even[j].astype(jnp.bfloat16)
                 send[t, g, to + 1] = odd[j].astype(jnp.bfloat16)
 
-            if (t, g) in ((2, 0), (3, 0)):
-                halo_pieces(12 + 10 * (t - 2) + 5 * u, 5)
-
-            def push(d):
-                to = q * (2 * pairs) + lax.rem(me + 1 + 3 * d, 2 * pairs)
-                direct = to != me
-                if (t, g) in RELAYED:
-                    direct = jnp.logical_and(direct, lax.rem(to // 2, 4) != z_two)
-
-                @pl.when(direct)
-                def _():
-                    out_copy(t, g, to).start()
-
-            repeat(2 * pairs, push)
+        def push(d):
+            step = lax.rem(11 * d + 5, PEERS)
+            far = lax.rem(step // 2, 4)
+            to = lax.rem(y + step // 8, 4) * 8 + lax.rem(z + far, 4) * 2 + lax.rem(core + step, 2)
+            direct = step != 0
+            if (t, g) in RELAYED:
+                direct = jnp.logical_and(direct, far != 2)
+
+            @pl.when(direct)
+            def _():
+                out_copy(t, g, to).start()
 
         repeat(2, body)
-        own_copy(t, g).start()
         if (t, g) in RELAYED:
             repeat(8, lambda d: relay_copy(RELAYED.index((t, g)), d).start())
+        repeat(PEERS, push)
+        own_copy(t, g).start()
 
     def sum_copy(t, to):
         return pltpu.make_async_remote_copy(
@@ -315,7 +313,7 @@
         own_sums(t).start()
 
     pl.semaphore_wait(barrier, PEERS + 1)
-    halo_pieces(0, 12)
+    halo_pieces(0, 32)
     for f in (2, 3):
         load(f, 0).wait()
         split(f, 4, 5)

time: 92.8 us -> 92.5 us (level)
  no operation moved by 1% of the time
where the time goes in v3:
time: 92.5 us; the launch traced here: 92.3 us
  Pallas kernels  92.1 us (100%)
    pallas_call x1, Pallas kernels, conv_call(): pl.pallas_call(functools.partial(conv_kernel, entries), out_shape=[jax.Sh...  86.1 us
    pallas_call x1, Pallas kernels, last_call(): pl.pallas_call(functools.partial(last_kernel, entries), out_shape=jax.Sha...  6.06 us

profile of v3, /device:TPU:1, one launch (start us, length us, event | category | flops | bytes accessed | tf_op | source)
XLA Modules:
  0.0 92.3 jit_solution(16774131008033482074)
XLA Ops:
  0.0 86.1 %conv.1 = (bf16[4,2,32,40,256]{4,3,2,1,0:T(8,128)(2,1)}, f32[4,32,2,256]{3,2,1,0:T(2,128)}, bf16[2,20,128,256]{3,2,1,0:T(8,128)(2,1)}) custom-call(s32[16]{0:T(128)} %clips.1, bf16[4,8,1280,128]{3,2,1,0:T(8,128)(2,1)} %frames.1, bf16[3,1152,256]{2,1,0:T(8,128)(2,1)} %bitcast.4, f32[1,256]{1,0:T(1,128)} %bitcast.5, f32[1,256]{1,0:T(1,128)} %bitcast.7), custom_call_target="tpu_custom_call" | custom-call | tf_op jit(solution)/shard_map/conv/pallas_call | solution.py:413
  86.1 6.1 %last.1 = bf16[4,20,128,256]{3,2,1,0:T(8,128)(2,1)} custom-call(bf16[4,2,32,40,256]{4,3,2,1,0:T(8,128)(2,1)} %get-tuple-element.8.got, f32[4,32,2,256]{3,2,1,0:T(2,128)} %get-tuple-element.9.got_sums, f32[1,256]{1,0:T(1,128)} %bitcast.6, f32[1,256]{1,0:T(1,128)} %bitcast.8, bf16[2,20,128,256]{3,2,1,0:T(8,128)(2,1)} %get-tuple-element.10.done), custom_call_target="tpu_custom_call" | custom-call | tf_op jit(solution)/shard_map/last/pallas_call | solution.py:492
